TPU v7x, 256 devices: a whole 4x4x8 slice. The times are simulated.
256 devices in a mesh: row: 64 (over x, z, core), col: 4 (over y).
Axes of the slice: x: 4, y: 4, z: 8, core: 2. Of those that a mesh axis runs over, the one named last changes fastest.
Arguments:
- cost_first: bfloat16 [8192, 102400], P('row', 'col'), may hold values from -15 to 15, as said below
- cost_second: bfloat16 [8192, 102400], P('row', 'col'), may hold values from -15 to 15, as said below
- factors: bfloat16 [102400, 128], P(('col', 'row')), may hold values from 0.25 to 4
- slab_factors: float32 [8192, 128], P('row'), may hold values from 0.25 to 4
- weights: float32 [64], replicated, may hold values from 0.5 to 2
Outputs:
- new_factors: float32 [8192, 128], P('row')
- marginal: float32 [64], replicated
Inputs may be any that keep to these rules, and one draw needn't show every extreme that they name: `cost_first`: whole numbers. `cost_second`: whole numbers.
All inputs are finite; a program needn't handle non-finite values.
Results may differ from a plain program's by a relative error of at most 0.0003.
Values may be sent and summed in bfloat16 or wider, within the bound.
A program may use at most 64 MiB of HBM per device.

v0:
```python
import math

import jax
import jax.numpy as jnp
from jax import lax
from jax.sharding import PartitionSpec as P

N = 102400


STEP = 1.0


def rank_terms(current, products, rank):
    high = lax.Precision.HIGHEST
    k_first = jnp.dot(current[:, :rank].T, products[:, :rank], precision=high)
    k_second = jnp.dot(current[:, rank:].T, products[:, rank:], precision=high)
    return jnp.concatenate([k_first, k_second], axis=1)


def normalized(current, moved):
    shifted = moved - jnp.max(moved, axis=1, keepdims=True)
    tilde = current * jnp.exp(STEP * shifted)
    return tilde / jnp.sum(tilde, axis=1, keepdims=True)


def advance(current, products, stats, weights, rank):
    high = lax.Precision.HIGHEST
    inverse = 1.0 / weights
    scale = 1.0 / math.sqrt(rank)
    move_first = (
        jnp.dot(products[:, :rank] * inverse, stats[:, rank:] * inverse[None, :], precision=high)
        * scale
    )
    move_second = (
        jnp.dot(products[:, rank:] * inverse, stats[:, :rank] * inverse[None, :], precision=high)
        * scale
    )
    first = normalized(current[:, :rank], move_first)
    second = normalized(current[:, rank:], move_second)
    return jnp.concatenate([first, second], axis=1)


def local(cost_first, cost_second, factors, slab_factors, weights):
    rank = weights.shape[0]
    rows = cost_first.shape[0]
    slab_total = rows * lax.axis_size("row")
    piece = lax.all_gather(factors, "row", axis=0, tiled=True)
    left = jnp.dot(cost_first, piece[:, :rank], preferred_element_type=jnp.float32)
    right = jnp.dot(cost_second, piece[:, rank:], preferred_element_type=jnp.float32)
    partial_value = jnp.concatenate([left, right], axis=1)
    partial_value = partial_value * (1.0 / (16.0 * math.sqrt(N)))
    stat_scale = 1.0 / math.sqrt(slab_total)
    stats = None
    products = lax.psum(partial_value, "col")
    stats = lax.psum(rank_terms(slab_factors, products, rank), "row") * stat_scale
    updated = advance(slab_factors, products, stats, weights, rank)
    totals = lax.psum(jnp.sum(updated, axis=0), "row")
    marginal = rank / (2.0 * slab_total) * (totals[:rank] + totals[rank:])
    return (updated, marginal)


def solution(mesh):
    placed = (P("row", "col"), P("row", "col"), P(("col", "row"), None), P("row", None), P())
    return jax.shard_map(
        local, mesh=mesh, in_specs=placed, out_specs=(P("row", None), P()), check_vma=False
    )
```

profile of v0, /device:TPU:1, one launch (start us, length us, event | category | flops | bytes accessed | tf_op | source)
XLA Modules:
  0.0 538.4 jit_solution(754033275861534209)
XLA Ops:
  7.2 0.0 all-gather.2.cloned.1.call-start
  7.2 0.7 all-gather.2.cloned.1.call-update
  7.9 0.0 all-reduce.2.cloned.1.call-start
  7.9 1.0 fusion.19
  8.9 87.4 %all-gather.2.cloned.1.call-done = bf16[25600,128]{1,0:T(8,128)(2,1)} async-done(((bf16[400,128]{1,0:T(8,128)(2,1)}), bf16[25600,128]{1,0:T(8,128)(2,1)}) %all-gather.2.cloned.1.call-update) | async-done | bytes 6553616 | tf_op jit(solution)/shard_map/all_gather | solution.py:48
  96.3 0.0 copy-start
  96.3 0.0 copy-start.1
  96.3 10.3 %fusion = f32[128,64]{0,1:T(8,128)S(1)} fusion(bf16[128,25600]{1,0:T(8,128)(2,1)} %param.6, bf16[25600,128]{1,0:T(8,128)(2,1)} %all-gather.2.cloned.1.call-done), kind=kOutput, calls=%fused_computation | convolution fusion | flops 419430400 | bytes 13139968 | tf_op jit(solution)/shard_map/dot_general | solution.py:50
  106.6 0.0 copy-done
  106.6 0.0 copy-done.1
  106.7 0.0 copy-start.3
  106.7 0.0 copy-start.2
  106.7 3.0 fusion.2
  109.7 0.6 maximum_multiply_fusion
  110.4 0.0 all-reduce.2.cloned.1.call-update
  110.4 0.0 copy-done.3
  110.4 0.1 copy.10
  110.5 0.1 copy.11
  110.5 40.1 %all-reduce.2.cloned.1.call-done = f32[128,128]{0,1:T(8,128)} async-done(((f32[128,128]{0,1:T(8,128)}), f32[128,128]{0,1:T(8,128)}) %all-reduce.2.cloned.1.call-update) | async-done | bytes 65552 | tf_op jit(solution)/shard_map/psum | solution.py:55
  150.7 0.0 copy-done.2
  150.7 1.1 convolution_bitcast_fusion
  151.8 1.0 convolution_bitcast_fusion.1
  152.8 0.1 pad_maximum_fusion.1
  152.9 246.0 %psum.22 = f32[64,128]{1,0:T(8,128)S(1)} all-reduce(f32[64,128]{1,0:T(8,128)S(1)} %pad_maximum_fusion.1), channel_id=1, replica_groups=mesh['row'=64,'col'=4] {'row'}, use_global_device_ids=true, to_apply=%region_1.0 | all-reduce | flops 8192 | bytes 65536 | tf_op jit(solution)/shard_map/psum | solution.py:56
  398.9 1.1 fusion.21
  400.0 1.0 fusion.20
  401.1 0.1 fusion.18
  401.2 0.7 copy.9
  402.0 129.0 %psum.23 = f32[128]{0:T(128)S(1)} all-reduce(f32[128]{0:T(128)S(1)} %get-tuple-element.4), channel_id=1, replica_groups=mesh['row'=64,'col'=4] {'row'}, use_global_device_ids=true, to_apply=%region_7.0 | all-reduce | flops 128 | bytes 1024 | tf_op jit(solution)/shard_map/psum | solution.py:58
  531.0 0.6 add_multiply_fusion
  (5 shorter events, 0.1 us)
Async XLA Ops:
  7.2 89.2 %all-gather.2.cloned.1.call-start = ((), (), s32[]{:S(2)}) async-start(), calls=%async_computation | async-start | bytes 6656000 | tf_op jit(solution)/shard_map/all_gather | solution.py:48
  7.9 142.8 %all-reduce.2.cloned.1.call-start = ((), (), s32[]{:S(2)}) async-start(), calls=%async_computation.1 | async-start | bytes 131072 | tf_op jit(solution)/shard_map/psum | solution.py:55
  96.3 10.3 %copy-start = (bf16[25600,128]{1,0:T(8,128)(2,1)S(1)}, bf16[25600,128]{1,0:T(8,128)(2,1)}, u32[]{:S(2)}) copy-start(bf16[25600,128]{1,0:T(8,128)(2,1)} %all-gather.2.cloned.1.call-done) | copy-start | bytes 19660804
  96.3 10.3 %copy-start.1 = (bf16[128,25600]{1,0:T(8,128)(2,1)S(1)}, bf16[128,25600]{1,0:T(8,128)(2,1)}, u32[]{:S(2)}) copy-start(bf16[128,25600]{1,0:T(8,128)(2,1)} %param.5) | copy-start | bytes 19660804
  106.7 3.7 copy-start.3
  106.7 44.0 %copy-start.2 = (f32[128,128]{1,0:T(8,128)S(1)}, f32[128,128]{1,0:T(8,128)}, u32[]{:S(2)}) copy-start(f32[128,128]{1,0:T(8,128)} %param.8) | copy-start | bytes 196612
Sparse Core Ops, SparseCore 0:
  10.7 85.5 all-gather.1
  110.5 40.1 all-reduce.1
where the time goes:
time: 539 us; the launch traced here: 538 us
  blocking collectives  375 us (70%)
  waiting for transfers between devices  128 us (24%)
  matrix products  17.6 us (3%)
  between operations  14.1 us (3%)
    psum x1, blocking collectives, local(): lax.psum(rank_terms(slab_factors, products, rank), 'row') * stat_scale  246 us
    psum x1, blocking collectives, local(): totals = lax.psum(jnp.sum(updated, axis=0), 'row')  129 us
    all_gather x1, waiting for transfers between devices, local(): piece = lax.all_gather(factors, 'row', axis=0, tiled=True)  87.4 us
    psum x1, waiting for transfers between devices, local(): products = lax.psum(partial_value, 'col')  40.1 us
  transfers between devices with their start and end apart: 2, of which 2 were waited for; matrix products, arithmetic and copies ran while one was open for 0% of the time, Pallas kernels for 0%

commit v1 on v0

v1 whole, which is shorter than its diff:
```python
import math

import jax
import jax.numpy as jnp
from jax import lax
from jax.experimental import pallas as pl
from jax.experimental.pallas import tpu as pltpu
from jax.sharding import PartitionSpec as P

MESH = pl.DeviceIdType.MESH
HIGH = lax.Precision.HIGHEST

NX, NY, NZ = 4, 4, 8
RANK = 64
LANES = 2 * RANK
ROWS = 128
DEEP = 400
BLOCKS = 64
SLOT = 512
N = 102400
SLAB = 8192

STEPS = (
    ((1, 0), (3, 0), (0, 1), (0, 7)),
    ((1, 7), (3, 7), (3, 1), (0, 6)),
    ((1, 1), (2, 0), (0, 2), (0, 5)),
    ((2, 7), (2, 1), (3, 2), (1, 6)),
    ((1, 5), (3, 6), (0, 3), (0, 4)),
    ((2, 6), (3, 5), (3, 3), (1, 4)),
    ((2, 5), (2, 2), (1, 2), (1, 3)),
    ((2, 4), (2, 3), (3, 4), None),
)
LINKS = ((1, 0), (-1, 0), (0, 1), (0, -1))
CHUNKS = ((0, 144), (144, 128), (272, 128))


def plan():
    when = {(0, 0): -1}
    for step, row in enumerate(STEPS):
        for offset in row:
            if offset is not None:
                when[offset] = step
    queues = []
    for link, (ux, uz) in enumerate(LINKS):
        queue = []
        for step, row in enumerate(STEPS):
            if row[link] is not None:
                ox, oz = row[link]
                source = ((ox - ux) % NX, (oz - uz) % NZ)
                assert when[source] < step
                for chunk in range(len(CHUNKS)):
                    queue.append((source, when[source], step, chunk))
        queues.append(queue)
    return queues


def kernel(
    cost_first, cost_second, factors, slab, weights, new, marginal,
    costs, slots, total, turned, prods, stat, scattered, crossed, gathered, sums,
    load_sem, own_sem, send_sem, ring_sem, twin_sem,
    small_send, scatter_sem, cross_sem, gather_sem, prod_sem, sum_sem,
):
    row = lax.axis_index("row")
    y = lax.axis_index("col")
    core = lax.rem(row, 2)
    z = lax.rem(row // 2, NZ)
    x = row // (2 * NZ)
    sign = 1 - 2 * core

    def device(dx, dy, dz, dc):
        xx = lax.rem(x + dx + NX, NX)
        yy = lax.rem(y + dy + NY, NY)
        zz = lax.rem(z + dz + NZ, NZ)
        cc = lax.rem(core + dc, 2)
        return ((xx * NZ + zz) * 2 + cc, yy)

    def block(offset, way, c):
        ox, oz = offset
        ox, oz = (ox - NX if ox > NX // 2 else ox), (oz - NZ if oz > NZ // 2 else oz)
        xx = lax.rem(x - way * ox + NX, NX)
        zz = lax.rem(z - way * oz + NZ, NZ)
        return (xx * NZ + zz) * 2 + c

    def rows_of(b, start, size):
        return pl.ds(pl.multiple_of(16 * lax.rem(b, 8) + start, 16), size)

    def remote(src, dst, send, recv, to):
        return pltpu.make_async_remote_copy(
            src_ref=src, dst_ref=dst, send_sem=send, recv_sem=recv,
            device_id=to, device_id_type=MESH,
        )

    load_first = pltpu.make_async_copy(cost_first, costs.at[pl.ds(0, ROWS)], load_sem.at[0])
    load_second = pltpu.make_async_copy(cost_second, costs.at[pl.ds(ROWS, ROWS)], load_sem.at[1])
    own_slot = slots.at[row, rows_of(row, 0, DEEP)]
    load_own = pltpu.make_async_copy(factors, own_slot, own_sem)

    barrier = pltpu.get_barrier_semaphore()
    pairs = [(dy, dc) for dy in range(NY) for dc in range(2) if (dy, dc) != (0, 0)]
    greeted = [device(ux, 0, uz, 0) for ux, uz in LINKS]
    greeted += [device(0, dy, 0, dc) for dy, dc in pairs]
    for to in greeted:
        pl.semaphore_signal(barrier, inc=1, device_id=to, device_id_type=MESH)
    load_own.start()
    load_first.start()
    load_second.start()
    pl.semaphore_wait(barrier, len(greeted))

    neighbour = [device(sign * ux, 0, sign * uz, 0) for ux, uz in LINKS]
    twin = device(0, 0, 0, 1)
    queues = plan()
    heads = [0] * len(LINKS)

    def send_ready(done_step, done_chunk):
        progress = True
        while progress:
            progress = False
            for link in range(len(LINKS)):
                if heads[link] < len(queues[link]):
                    source, came, step, chunk = queues[link][heads[link]]
                    if (came, chunk) <= (done_step, done_chunk) or came < 0:
                        start, size = CHUNKS[chunk]
                        b = block(source, sign, core)
                        here = slots.at[b, rows_of(b, start, size)]
                        src = factors.at[pl.ds(start, size)] if came < 0 else here
                        remote(
                            src, here, send_sem.at[0],
                            ring_sem.at[(step * len(LINKS) + link) * len(CHUNKS) + chunk],
                            neighbour[link],
                        ).start()
                        heads[link] += 1
                        progress = True

    send_ready(-1, len(CHUNKS))
    remote(factors, own_slot, send_sem.at[0], twin_sem.at[0], twin).start()

    blank = jnp.zeros((16, LANES), jnp.bfloat16)

    def clear(group, carry):
        for m in range(8):
            for i in range(7):
                at = 16 * (i if i < m else DEEP // 16 + i)
                slots[group * 8 + m, pl.ds(at, 16), :] = blank
        return carry

    lax.fori_loop(0, BLOCKS // 8, clear, 0)
    total[...] = jnp.zeros_like(total)
    turned[...] = slab[...].T

    def multiply(blocks):
        def one(j, carry):
            b = blocks[0]
            for k in range(1, len(blocks)):
                b = jnp.where(j == k, blocks[k], b)
            at = pl.multiple_of(DEEP * b - 16 * lax.rem(b, 8), 128)
            total[...] += jnp.dot(
                costs[:, pl.ds(at, SLOT)], slots[b], preferred_element_type=jnp.float32
            )
            return carry

        lax.fori_loop(0, len(blocks), one, 0)

    def twin_wait(index, b):
        ref = slots.at[b, rows_of(b, 0, DEEP)]
        remote(ref, ref, send_sem.at[0], twin_sem.at[index], twin).wait_recv()

    mine, theirs = [((0, 0), 0)], [((0, 0), 0)]
    count = 1
    for step, offsets in enumerate(STEPS):
        arrived = []
        for chunk, (start, size) in enumerate(CHUNKS):
            for link, offset in enumerate(offsets):
                if offset is not None:
                    b = block(offset, sign, core)
                    ref = slots.at[b, rows_of(b, start, size)]
                    remote(
                        ref, ref, send_sem.at[0],
                        ring_sem.at[(step * len(LINKS) + link) * len(CHUNKS) + chunk],
                        neighbour[link],
                    ).wait_recv()
            send_ready(step, chunk)
            if chunk == len(CHUNKS) - 1:
                for offset in offsets:
                    if offset is not None:
                        b = block(offset, sign, core)
                        whole = slots.at[b, rows_of(b, 0, DEEP)]
                        remote(whole, whole, send_sem.at[0], twin_sem.at[count], twin).start()
                        arrived.append((offset, count))
                        count += 1
            if chunk == 0:
                if step == 0:
                    load_own.wait()
                    load_first.wait()
                    load_second.wait()
                multiply([block(offset, sign, core) for offset, _ in mine])
            if chunk == 1:
                for offset, index in theirs:
                    twin_wait(index, block(offset, -sign, 1 - core))
                multiply([block(offset, -sign, 1 - core) for offset, _ in theirs])
        mine = theirs = arrived
    multiply([block(offset, sign, core) for offset, _ in mine])
    for offset, index in theirs:
        twin_wait(index, block(offset, -sign, 1 - core))
    multiply([block(offset, -sign, 1 - core) for offset, _ in theirs])

    half = lax.broadcasted_iota(jnp.int32, (1, LANES), 1) < RANK
    part = jnp.where(half, total[0:ROWS, :], total[ROWS:, :]) * (1.0 / (16.0 * math.sqrt(N)))
    prods[y] = part
    terms = jnp.dot(turned[...], part, precision=HIGH, preferred_element_type=jnp.float32)
    stat[...] = jnp.where(half, terms[0:RANK, :], terms[RANK:, :])

    me = y * 2 + core
    scattered[me] = stat[pl.ds(pl.multiple_of(8 * me, 8), 8), :]
    for dy, dc in pairs:
        to = device(0, dy, 0, dc)
        g = to[1] * 2 + lax.rem(to[0], 2)
        remote(
            stat.at[pl.ds(pl.multiple_of(8 * g, 8), 8)], scattered.at[me],
            small_send.at[0], scatter_sem.at[0], to,
        ).start()
    seven = scattered.at[pl.ds(0, len(pairs))]
    pltpu.make_async_copy(seven, seven, scatter_sem.at[0]).wait()
    place = x * NZ + z
    piece = scattered[0]
    for g in range(1, 8):
        piece = piece + scattered[g]
    crossed[place] = piece
    far = [
        (dx, dz) for dz in (4, 3, 5, 2, 6, 1, 7, 0) for dx in (2, 1, 3, 0) if (dx, dz) != (0, 0)
    ]
    for dx, dz in far:
        remote(
            crossed.at[place], crossed.at[place], small_send.at[1], cross_sem.at[0],
            device(dx, 0, dz, 0),
        ).start()
    for dy in (2, 1, 3):
        remote(
            prods.at[y], prods.at[y], small_send.at[2], prod_sem.at[0], device(0, dy, 0, 0)
        ).start()
    others = crossed.at[pl.ds(0, len(far))]
    pltpu.make_async_copy(others, others, cross_sem.at[0]).wait()
    piece = jnp.sum(crossed[...], axis=0)
    mine_rows = pl.ds(pl.multiple_of(8 * me, 8), 8)
    gathered[mine_rows, :] = piece
    for dy, dc in pairs:
        remote(
            gathered.at[mine_rows], gathered.at[mine_rows], small_send.at[3], gather_sem.at[0],
            device(0, dy, 0, dc),
        ).start()
    three = prods.at[pl.ds(0, NY - 1)]
    pltpu.make_async_copy(three, three, prod_sem.at[0]).wait()
    inverse = 1.0 / weights[...]
    inverse = jnp.concatenate([inverse, inverse], axis=1)
    product = ((prods[0] + prods[1]) + prods[2]) + prods[3]
    product = product * inverse
    most = gathered.at[pl.ds(0, 8 * len(pairs))]
    pltpu.make_async_copy(most, most, gather_sem.at[0]).wait()
    stats = gathered[...] * (1.0 / math.sqrt(SLAB))
    swapped = jnp.concatenate([stats[:, RANK:], stats[:, :RANK]], axis=1) * inverse
    both = jnp.concatenate(
        [jnp.where(half, swapped, 0.0), jnp.where(half, 0.0, swapped)], axis=0
    )
    move = jnp.dot(product, both, precision=HIGH, preferred_element_type=jnp.float32)
    move = move * (1.0 / math.sqrt(RANK))
    low = jnp.max(jnp.where(half, move, -jnp.inf), axis=1, keepdims=True)
    high = jnp.max(jnp.where(half, -jnp.inf, move), axis=1, keepdims=True)
    tilde = slab[...] * jnp.exp(move - jnp.where(half, low, high))
    low = jnp.sum(jnp.where(half, tilde, 0.0), axis=1, keepdims=True)
    high = jnp.sum(jnp.where(half, 0.0, tilde), axis=1, keepdims=True)
    updated = tilde / jnp.where(half, low, high)
    sums[row] = jnp.sum(updated, axis=0, keepdims=True)
    for dx, dz in far + [(0, 0)]:
        for dc in (0, 1):
            if (dx, dz, dc) != (0, 0, 0):
                remote(
                    sums.at[row], sums.at[row], small_send.at[4], sum_sem.at[0],
                    device(dx, 0, dz, dc),
                ).start()
    new[...] = updated

    rest = sums.at[pl.ds(0, BLOCKS - 1)]
    sent = slots.at[pl.ds(0, BLOCKS - 1), pl.ds(0, DEEP)]
    pltpu.make_async_copy(sent, sent, send_sem.at[0]).wait()
    pltpu.make_async_copy(seven, seven, small_send.at[0]).wait()
    pltpu.make_async_copy(others, others, small_send.at[1]).wait()
    pltpu.make_async_copy(three, three, small_send.at[2]).wait()
    pltpu.make_async_copy(most, most, small_send.at[3]).wait()
    pltpu.make_async_copy(rest, rest, sum_sem.at[0]).wait()
    sums_all = jnp.sum(sums[...], axis=0)
    marginal[...] = (RANK / (2.0 * SLAB)) * (sums_all[:, :RANK] + sums_all[:, RANK:])
    pltpu.make_async_copy(rest, rest, small_send.at[4]).wait()


def local(cost_first, cost_second, factors, slab_factors, weights):
    vmem = pl.BlockSpec(memory_space=pltpu.VMEM)
    hbm = pl.BlockSpec(memory_space=pl.ANY)
    f32 = jnp.float32
    dma = pltpu.SemaphoreType.DMA
    new, marginal = pl.pallas_call(
        kernel,
        out_shape=(
            jax.ShapeDtypeStruct((ROWS, LANES), f32),
            jax.ShapeDtypeStruct((1, RANK), f32),
        ),
        in_specs=[hbm, hbm, hbm, vmem, vmem],
        out_specs=(vmem, vmem),
        scratch_shapes=[
            pltpu.VMEM((2 * ROWS, BLOCKS * DEEP), jnp.bfloat16),
            pltpu.VMEM((BLOCKS, SLOT, LANES), jnp.bfloat16),
            pltpu.VMEM((2 * ROWS, LANES), f32),
            pltpu.VMEM((LANES, ROWS), f32),
            pltpu.VMEM((NY, ROWS, LANES), f32),
            pltpu.VMEM((RANK, LANES), f32),
            pltpu.VMEM((8, 8, LANES), f32),
            pltpu.VMEM((NX * NZ, 8, LANES), f32),
            pltpu.VMEM((RANK, LANES), f32),
            pltpu.VMEM((BLOCKS, 1, LANES), f32),
            dma((2,)),
            dma,
            dma((1,)),
            dma((len(STEPS) * len(LINKS) * len(CHUNKS),)),
            dma((NX * NZ,)),
            dma((5,)),
            dma((1,)),
            dma((1,)),
            dma((1,)),
            dma((1,)),
            dma((1,)),
        ],
        compiler_params=pltpu.CompilerParams(
            collective_id=0, has_side_effects=True, vmem_limit_bytes=44 << 20
        ),
    )(cost_first, cost_second, factors, slab_factors, weights.reshape(1, RANK))
    return new, marginal.reshape(RANK)


def solution(mesh):
    placed = (P("row", "col"), P("row", "col"), P(("col", "row"), None), P("row", None), P())
    return jax.shard_map(
        local, mesh=mesh, in_specs=placed, out_specs=(P("row", None), P()), check_vma=False
    )
```

time: 539 us -> 66.4 us (0.12)
  blocking collectives: 375 us -> 0 us
  waiting for transfers between devices: 128 us -> 0 us
  Pallas kernels: 0 us -> 59.1 us
  matrix products: 17.6 us -> 0 us
  between operations: 14.1 us -> 0.65 us
    psum x2 -> x0, blocking collectives: 375 us -> none  [the longest x1 246 us: local(): lax.psum(rank_terms(slab_factors, products, rank), 'row') * stat_scale]
    all_gather x1 -> x0, waiting for transfers between devices: 87.4 us -> none  [local(): piece = lax.all_gather(factors, 'row', axis=0, tiled=True)]
    pallas_call x0 -> x1, Pallas kernels: none -> 59.1 us  [local(): pl.pallas_call(kernel, out_shape=(jax.ShapeDtypeStruct((ROWS, LANES), f32...]
    psum x1 -> x0, waiting for transfers between devices: 40.1 us -> none  [local(): products = lax.psum(partial_value, 'col')]
    dot_general x6 -> x0, matrix products: 17.6 us -> none  [the longest x1 10.3 us: local(): jnp.dot(cost_second, piece[:, rank:], preferred_element_type=jnp.float32)]
  transfers between devices with their start and end apart: 2 -> 0, of which waited for: 2 -> 0; matrix products, arithmetic and copies ran while one was open for 0% -> 0% of each run, Pallas kernels for 0% -> 0%
where the time goes in v1:
time: 66.4 us; the launch traced here: 66.2 us
  Pallas kernels  59.1 us (89%)
  local copies, waits for them, and re-layouts  6.38 us (10%)
    pallas_call x1, Pallas kernels, local(): pl.pallas_call(kernel, out_shape=(jax.ShapeDtypeStruct((ROWS, LANES), f32...  59.1 us
    unnamed x10, local copies, waits for them, and re-layouts  6.38 us

profile of v1, /device:TPU:1, one launch (start us, length us, event | category | flops | bytes accessed | tf_op | source)
XLA Modules:
  0.0 66.2 jit_solution(1585704519951442199)
XLA Ops:
  0.6 0.0 copy-start
  0.6 2.9 %copy-done = bf16[128,25600]{1,0:T(8,128)(2,1)S(1)} copy-done((bf16[128,25600]{1,0:T(8,128)(2,1)S(1)}, bf16[128,25600]{1,0:T(8,128)(2,1)}, u32[]{:S(2)}) %copy-start) | copy-done | bytes 6553624
  3.5 0.0 copy-start.1
  3.5 0.9 %copy-done.1 = bf16[400,128]{1,0:T(8,128)(2,1)S(1)} copy-done((bf16[400,128]{1,0:T(8,128)(2,1)S(1)}, bf16[400,128]{1,0:T(8,128)(2,1)}, u32[]{:S(2)}) %copy-start.1) | copy-done | bytes 102424
  4.4 0.0 copy-start.2
  4.4 0.8 %copy-done.2 = f32[128,128]{1,0:T(8,128)S(1)} copy-done((f32[128,128]{1,0:T(8,128)S(1)}, f32[128,128]{1,0:T(8,128)}, u32[]{:S(2)}) %copy-start.2) | copy-done | bytes 65560
  5.2 0.0 copy-start.3
  5.2 0.7 copy-done.3
  5.9 59.1 %shard_map.68 = (f32[128,128]{1,0:T(8,128)S(1)}, f32[1,64]{1,0:T(1,128)S(1)}) custom-call(bf16[128,25600]{1,0:T(8,128)(2,1)S(1)} %copy-done, bf16[128,25600]{1,0:T(8,128)(2,1)} %cost_second.1, bf16[400,128]{1,0:T(8,128)(2,1)S(1)} %copy-done.1, f32[128,128]{1,0:T(8,128)S(1)} %copy-done.2, f32[1,64]{1,0:T(1,128)S(1)} %bitcast.2), custom_call_target="tpu_custom_call" | custom-call | tf_op jit(solution)/shard_map/pallas_call | solution.py:299
  65.0 0.6 copy.9
  65.7 0.5 copy.10
Async XLA Ops:
  0.6 2.9 %copy-start = (bf16[128,25600]{1,0:T(8,128)(2,1)S(1)}, bf16[128,25600]{1,0:T(8,128)(2,1)}, u32[]{:S(2)}) copy-start(bf16[128,25600]{1,0:T(8,128)(2,1)} %cost_first.1) | copy-start | bytes 19660804
  3.5 0.9 %copy-start.1 = (bf16[400,128]{1,0:T(8,128)(2,1)S(1)}, bf16[400,128]{1,0:T(8,128)(2,1)}, u32[]{:S(2)}) copy-start(bf16[400,128]{1,0:T(8,128)(2,1)} %factors.1) | copy-start | bytes 307204
  4.4 0.8 %copy-start.2 = (f32[128,128]{1,0:T(8,128)S(1)}, f32[128,128]{1,0:T(8,128)}, u32[]{:S(2)}) copy-start(f32[128,128]{1,0:T(8,128)} %slab.1) | copy-start | bytes 196612
  5.2 0.7 copy-start.3

commit v2 on v1

--- a/solution.py
+++ b/solution.py
@@ -55,9 +55,10 @@
 
 
 def kernel(
-    cost_first, cost_second, factors, slab, weights, new, marginal,
-    costs, slots, total, turned, prods, stat, scattered, crossed, gathered, sums,
-    load_sem, own_sem, send_sem, ring_sem, twin_sem,
+    cost_first, cost_second, factors, slab_in, weights_in, new, marginal,
+    slab, twin_slab, weights, costs, twins, slots, total, turned, halves, outgoing, prods,
+    stat, scattered, crossed, gathered, sums,
+    load_sem, own_sem, send_sem, ring_sem, twin_sem, slab_sem, half_sem,
     small_send, scatter_sem, cross_sem, gather_sem, prod_sem, sum_sem,
 ):
     row = lax.axis_index("row")
@@ -84,6 +85,9 @@
     def rows_of(b, start, size):
         return pl.ds(pl.multiple_of(16 * lax.rem(b, 8) + start, 16), size)
 
+    def column(b):
+        return pl.multiple_of(DEEP * b - 16 * lax.rem(b, 8), 128)
+
     def remote(src, dst, send, recv, to):
         return pltpu.make_async_remote_copy(
             src_ref=src, dst_ref=dst, send_sem=send, recv_sem=recv,
@@ -92,8 +96,11 @@
 
     load_first = pltpu.make_async_copy(cost_first, costs.at[pl.ds(0, ROWS)], load_sem.at[0])
     load_second = pltpu.make_async_copy(cost_second, costs.at[pl.ds(ROWS, ROWS)], load_sem.at[1])
-    own_slot = slots.at[row, rows_of(row, 0, DEEP)]
+    place = x * NZ + z
+    own_slot = slots.at[place, rows_of(row, 0, DEEP)]
     load_own = pltpu.make_async_copy(factors, own_slot, own_sem)
+    load_slab = pltpu.make_async_copy(slab_in, slab, load_sem.at[2])
+    load_weights = pltpu.make_async_copy(weights_in, weights, load_sem.at[3])
 
     barrier = pltpu.get_barrier_semaphore()
     pairs = [(dy, dc) for dy in range(NY) for dc in range(2) if (dy, dc) != (0, 0)]
@@ -101,6 +108,8 @@
     greeted += [device(0, dy, 0, dc) for dy, dc in pairs]
     for to in greeted:
         pl.semaphore_signal(barrier, inc=1, device_id=to, device_id_type=MESH)
+    load_slab.start()
+    load_weights.start()
     load_own.start()
     load_first.start()
     load_second.start()
@@ -121,7 +130,7 @@
                     if (came, chunk) <= (done_step, done_chunk) or came < 0:
                         start, size = CHUNKS[chunk]
                         b = block(source, sign, core)
-                        here = slots.at[b, rows_of(b, start, size)]
+                        here = slots.at[b // 2, rows_of(b, start, size)]
                         src = factors.at[pl.ds(start, size)] if came < 0 else here
                         remote(
                             src, here, send_sem.at[0],
@@ -132,81 +141,93 @@
                         progress = True
 
     send_ready(-1, len(CHUNKS))
-    remote(factors, own_slot, send_sem.at[0], twin_sem.at[0], twin).start()
+
+    order = [(0, 0)] + [offset for row_of in STEPS for offset in row_of if offset is not None]
+
+    def lend(indices):
+        for k in indices:
+            if k < len(order):
+                b = block(order[k], -sign, 1 - core)
+                at = pl.ds(column(b), SLOT)
+                for part, cost in enumerate((cost_first, cost_second)):
+                    remote(
+                        cost.at[:, at], twins.at[k, pl.ds(part * ROWS, ROWS)],
+                        send_sem.at[1], twin_sem.at[k], twin,
+                    ).start()
+
+    lend(range(0, 9))
+    remote(slab_in, twin_slab, send_sem.at[2], slab_sem, twin).start()
 
     blank = jnp.zeros((16, LANES), jnp.bfloat16)
 
     def clear(group, carry):
-        for m in range(8):
+        for j in range(4):
+            m = 2 * j + core
             for i in range(7):
-                at = 16 * (i if i < m else DEEP // 16 + i)
-                slots[group * 8 + m, pl.ds(at, 16), :] = blank
+                at = pl.multiple_of(16 * (i + jnp.where(i < m, 0, DEEP // 16)), 16)
+                slots[group * 4 + j, pl.ds(at, 16), :] = blank
         return carry
 
-    lax.fori_loop(0, BLOCKS // 8, clear, 0)
+    lax.fori_loop(0, NX * NZ // 4, clear, 0)
     total[...] = jnp.zeros_like(total)
-    turned[...] = slab[...].T
-
-    def multiply(blocks):
+    load_slab.wait()
+    load_weights.wait()
+    turned[:, 0:ROWS] = slab[...].T
+
+    def multiply(first, offsets):
+        blocks = [block(offset, sign, core) for offset in offsets]
+        for k in range(len(blocks)):
+            ref = twins.at[first + k]
+            pltpu.make_async_copy(ref, ref, twin_sem.at[first + k]).wait()
+
         def one(j, carry):
             b = blocks[0]
             for k in range(1, len(blocks)):
                 b = jnp.where(j == k, blocks[k], b)
-            at = pl.multiple_of(DEEP * b - 16 * lax.rem(b, 8), 128)
-            total[...] += jnp.dot(
-                costs[:, pl.ds(at, SLOT)], slots[b], preferred_element_type=jnp.float32
-            )
+            left = jnp.concatenate([costs[:, pl.ds(column(b), SLOT)], twins[first + j]], axis=0)
+            total[...] += jnp.dot(left, slots[b // 2], preferred_element_type=jnp.float32)
             return carry
 
         lax.fori_loop(0, len(blocks), one, 0)
 
-    def twin_wait(index, b):
-        ref = slots.at[b, rows_of(b, 0, DEEP)]
-        remote(ref, ref, send_sem.at[0], twin_sem.at[index], twin).wait_recv()
-
-    mine, theirs = [((0, 0), 0)], [((0, 0), 0)]
-    count = 1
+    ready, first = [(0, 0)], 0
     for step, offsets in enumerate(STEPS):
-        arrived = []
         for chunk, (start, size) in enumerate(CHUNKS):
             for link, offset in enumerate(offsets):
                 if offset is not None:
                     b = block(offset, sign, core)
-                    ref = slots.at[b, rows_of(b, start, size)]
+                    ref = slots.at[b // 2, rows_of(b, start, size)]
                     remote(
                         ref, ref, send_sem.at[0],
                         ring_sem.at[(step * len(LINKS) + link) * len(CHUNKS) + chunk],
                         neighbour[link],
                     ).wait_recv()
             send_ready(step, chunk)
-            if chunk == len(CHUNKS) - 1:
-                for offset in offsets:
-                    if offset is not None:
-                        b = block(offset, sign, core)
-                        whole = slots.at[b, rows_of(b, 0, DEEP)]
-                        remote(whole, whole, send_sem.at[0], twin_sem.at[count], twin).start()
-                        arrived.append((offset, count))
-                        count += 1
             if chunk == 0:
+                lend(range(4 * step + 9, 4 * step + 13))
                 if step == 0:
                     load_own.wait()
                     load_first.wait()
                     load_second.wait()
-                multiply([block(offset, sign, core) for offset, _ in mine])
-            if chunk == 1:
-                for offset, index in theirs:
-                    twin_wait(index, block(offset, -sign, 1 - core))
-                multiply([block(offset, -sign, 1 - core) for offset, _ in theirs])
-        mine = theirs = arrived
-    multiply([block(offset, sign, core) for offset, _ in mine])
-    for offset, index in theirs:
-        twin_wait(index, block(offset, -sign, 1 - core))
-    multiply([block(offset, -sign, 1 - core) for offset, _ in theirs])
+                multiply(first, ready)
+                first += len(ready)
+        ready = [offset for offset in offsets if offset is not None]
+    multiply(first, ready)
 
     half = lax.broadcasted_iota(jnp.int32, (1, LANES), 1) < RANK
-    part = jnp.where(half, total[0:ROWS, :], total[ROWS:, :]) * (1.0 / (16.0 * math.sqrt(N)))
-    prods[y] = part
-    terms = jnp.dot(turned[...], part, precision=HIGH, preferred_element_type=jnp.float32)
+    scale = 1.0 / (16.0 * math.sqrt(N))
+    part = jnp.where(half, total[0:ROWS, :], total[ROWS : 2 * ROWS, :]) * scale
+    lent = jnp.where(half, total[2 * ROWS : 3 * ROWS, :], total[3 * ROWS :, :]) * scale
+    outgoing[...] = lent
+    hand = remote(outgoing, halves.at[core], small_send.at[5], half_sem, twin)
+    hand.start()
+    halves[core] = part
+    remote(slab_in, twin_slab, send_sem.at[2], slab_sem, twin).wait_recv()
+    turned[:, ROWS:] = twin_slab[...].T
+    terms = jnp.dot(
+        turned[...], jnp.concatenate([part, lent], axis=0), precision=HIGH,
+        preferred_element_type=jnp.float32,
+    )
     stat[...] = jnp.where(half, terms[0:RANK, :], terms[RANK:, :])
 
     me = y * 2 + core
@@ -218,9 +239,14 @@
             stat.at[pl.ds(pl.multiple_of(8 * g, 8), 8)], scattered.at[me],
             small_send.at[0], scatter_sem.at[0], to,
         ).start()
+    hand.wait()
+    prods[y] = halves[0] + halves[1]
+    for dy in (2, 1, 3):
+        remote(
+            prods.at[y], prods.at[y], small_send.at[2], prod_sem.at[0], device(0, dy, 0, 0)
+        ).start()
     seven = scattered.at[pl.ds(0, len(pairs))]
     pltpu.make_async_copy(seven, seven, scatter_sem.at[0]).wait()
-    place = x * NZ + z
     piece = scattered[0]
     for g in range(1, 8):
         piece = piece + scattered[g]
@@ -232,10 +258,6 @@
         remote(
             crossed.at[place], crossed.at[place], small_send.at[1], cross_sem.at[0],
             device(dx, 0, dz, 0),
-        ).start()
-    for dy in (2, 1, 3):
-        remote(
-            prods.at[y], prods.at[y], small_send.at[2], prod_sem.at[0], device(0, dy, 0, 0)
         ).start()
     others = crossed.at[pl.ds(0, len(far))]
     pltpu.make_async_copy(others, others, cross_sem.at[0]).wait()
@@ -267,8 +289,8 @@
     tilde = slab[...] * jnp.exp(move - jnp.where(half, low, high))
     low = jnp.sum(jnp.where(half, tilde, 0.0), axis=1, keepdims=True)
     high = jnp.sum(jnp.where(half, 0.0, tilde), axis=1, keepdims=True)
-    updated = tilde / jnp.where(half, low, high)
-    sums[row] = jnp.sum(updated, axis=0, keepdims=True)
+    result = tilde / jnp.where(half, low, high)
+    sums[row] = jnp.sum(result, axis=0, keepdims=True)
     for dx, dz in far + [(0, 0)]:
         for dc in (0, 1):
             if (dx, dz, dc) != (0, 0, 0):
@@ -276,11 +298,13 @@
                     sums.at[row], sums.at[row], small_send.at[4], sum_sem.at[0],
                     device(dx, 0, dz, dc),
                 ).start()
-    new[...] = updated
+    new[...] = result
 
     rest = sums.at[pl.ds(0, BLOCKS - 1)]
-    sent = slots.at[pl.ds(0, BLOCKS - 1), pl.ds(0, DEEP)]
+    sent = slots.at[pl.ds(0, NX * NZ - 1), pl.ds(0, DEEP)]
     pltpu.make_async_copy(sent, sent, send_sem.at[0]).wait()
+    pltpu.make_async_copy(twins, twins, send_sem.at[1]).wait()
+    remote(slab_in, twin_slab, send_sem.at[2], slab_sem, twin).wait_send()
     pltpu.make_async_copy(seven, seven, small_send.at[0]).wait()
     pltpu.make_async_copy(others, others, small_send.at[1]).wait()
     pltpu.make_async_copy(three, three, small_send.at[2]).wait()
@@ -291,36 +315,54 @@
     pltpu.make_async_copy(rest, rest, small_send.at[4]).wait()
 
 
+def finish(new_in, marginal_in, new, marginal, sems):
+    first = pltpu.make_async_copy(new_in, new, sems.at[0])
+    second = pltpu.make_async_copy(marginal_in, marginal, sems.at[1])
+    first.start()
+    second.start()
+    first.wait()
+    second.wait()
+
+
 def local(cost_first, cost_second, factors, slab_factors, weights):
+    hbm = pl.BlockSpec(memory_space=pltpu.HBM)
     vmem = pl.BlockSpec(memory_space=pltpu.VMEM)
-    hbm = pl.BlockSpec(memory_space=pl.ANY)
-    f32 = jnp.float32
+    f32, bf16 = jnp.float32, jnp.bfloat16
     dma = pltpu.SemaphoreType.DMA
+    shapes = (
+        jax.ShapeDtypeStruct((ROWS, LANES), f32),
+        jax.ShapeDtypeStruct((1, RANK), f32),
+    )
     new, marginal = pl.pallas_call(
         kernel,
-        out_shape=(
-            jax.ShapeDtypeStruct((ROWS, LANES), f32),
-            jax.ShapeDtypeStruct((1, RANK), f32),
-        ),
-        in_specs=[hbm, hbm, hbm, vmem, vmem],
+        out_shape=tuple(pltpu.VMEM(shape.shape, shape.dtype) for shape in shapes),
+        in_specs=[hbm] * 5,
         out_specs=(vmem, vmem),
         scratch_shapes=[
-            pltpu.VMEM((2 * ROWS, BLOCKS * DEEP), jnp.bfloat16),
-            pltpu.VMEM((BLOCKS, SLOT, LANES), jnp.bfloat16),
-            pltpu.VMEM((2 * ROWS, LANES), f32),
-            pltpu.VMEM((LANES, ROWS), f32),
+            pltpu.VMEM((ROWS, LANES), f32),
+            pltpu.VMEM((ROWS, LANES), f32),
+            pltpu.VMEM((1, RANK), f32),
+            pltpu.VMEM((2 * ROWS, BLOCKS * DEEP), bf16),
+            pltpu.VMEM((NX * NZ, 2 * ROWS, SLOT), bf16),
+            pltpu.VMEM((NX * NZ, SLOT, LANES), bf16),
+            pltpu.VMEM((4 * ROWS, LANES), f32),
+            pltpu.VMEM((LANES, 2 * ROWS), f32),
+            pltpu.VMEM((2, ROWS, LANES), f32),
+            pltpu.VMEM((ROWS, LANES), f32),
             pltpu.VMEM((NY, ROWS, LANES), f32),
             pltpu.VMEM((RANK, LANES), f32),
             pltpu.VMEM((8, 8, LANES), f32),
             pltpu.VMEM((NX * NZ, 8, LANES), f32),
             pltpu.VMEM((RANK, LANES), f32),
             pltpu.VMEM((BLOCKS, 1, LANES), f32),
-            dma((2,)),
+            dma((4,)),
             dma,
-            dma((1,)),
+            dma((3,)),
             dma((len(STEPS) * len(LINKS) * len(CHUNKS),)),
             dma((NX * NZ,)),
-            dma((5,)),
+            dma,
+            dma,
+            dma((6,)),
             dma((1,)),
             dma((1,)),
             dma((1,)),
@@ -328,9 +370,17 @@
             dma((1,)),
         ],
         compiler_params=pltpu.CompilerParams(
-            collective_id=0, has_side_effects=True, vmem_limit_bytes=44 << 20
+            collective_id=0, has_side_effects=True, vmem_limit_bytes=60 << 20
         ),
     )(cost_first, cost_second, factors, slab_factors, weights.reshape(1, RANK))
+    new, marginal = pl.pallas_call(
+        finish,
+        out_shape=shapes,
+        in_specs=[vmem] * 2,
+        out_specs=(hbm, hbm),
+        scratch_shapes=[dma((2,))],
+        compiler_params=pltpu.CompilerParams(vmem_limit_bytes=1 << 20),
+    )(new, marginal)
     return new, marginal.reshape(RANK)
 
 

time: 66.4 us -> 58.7 us (0.88)
  local copies, waits for them, and re-layouts: 6.38 us -> 0 us
  Pallas kernels: 59.1 us -> 57.9 us
    unnamed x10 -> x0, local copies, waits for them, and re-layouts: 6.38 us -> none
    pallas_call x1 -> x2, Pallas kernels: 59.1 us -> 57.9 us  [the longest x1 57.3 us: local(): pl.pallas_call(kernel, out_shape=tuple((pltpu.VMEM(shape.shape, shape.dty...]
where the time goes in v2:
time: 58.7 us; the launch traced here: 58.6 us
  Pallas kernels  57.9 us (99%)
  between operations  0.64 us (1%)
    pallas_call x1, Pallas kernels, local(): pl.pallas_call(kernel, out_shape=tuple((pltpu.VMEM(shape.shape, shape.dty...  57.3 us

profile of v2, /device:TPU:1, one launch (start us, length us, event | category | flops | bytes accessed | tf_op | source)
XLA Modules:
  0.0 58.6 jit_solution(5590929852179204571)
XLA Ops:
  0.6 57.3 %shard_map.68 = (f32[128,128]{1,0:T(8,128)S(1)}, f32[1,64]{1,0:T(1,128)S(1)}) custom-call(bf16[128,25600]{1,0:T(8,128)(2,1)} %cost_first.1, bf16[128,25600]{1,0:T(8,128)(2,1)} %cost_second.1, bf16[400,128]{1,0:T(8,128)(2,1)} %factors.1, f32[128,128]{1,0:T(8,128)} %slab_in.1, f32[1,64]{1,0:T(1,128)} %bitcast.2), custom_call_target="tpu_custom_call" | custom-call | tf_op jit(solution)/shard_map/pallas_call | solution.py:336
  57.9 0.7 %shard_map.69 = (f32[128,128]{1,0:T(8,128)}, f32[1,64]{1,0:T(1,128)}) custom-call(f32[128,128]{1,0:T(8,128)S(1)} %get-tuple-element.6.new_in, f32[1,64]{1,0:T(1,128)S(1)} %get-tuple-element.7.marginal_in), custom_call_target="tpu_custom_call" | custom-call | tf_op jit(solution)/shard_map/pallas_call | solution.py:376

commit v3 on v2

--- a/solution.py
+++ b/solution.py
@@ -20,38 +20,37 @@
 N = 102400
 SLAB = 8192
 
-STEPS = (
-    ((1, 0), (3, 0), (0, 1), (0, 7)),
-    ((1, 7), (3, 7), (3, 1), (0, 6)),
-    ((1, 1), (2, 0), (0, 2), (0, 5)),
-    ((2, 7), (2, 1), (3, 2), (1, 6)),
-    ((1, 5), (3, 6), (0, 3), (0, 4)),
-    ((2, 6), (3, 5), (3, 3), (1, 4)),
-    ((2, 5), (2, 2), (1, 2), (1, 3)),
-    ((2, 4), (2, 3), (3, 4), None),
-)
+AHEAD = 9
 LINKS = ((1, 0), (-1, 0), (0, 1), (0, -1))
 CHUNKS = ((0, 144), (144, 128), (272, 128))
-
-
-def plan():
-    when = {(0, 0): -1}
-    for step, row in enumerate(STEPS):
-        for offset in row:
-            if offset is not None:
-                when[offset] = step
-    queues = []
-    for link, (ux, uz) in enumerate(LINKS):
-        queue = []
-        for step, row in enumerate(STEPS):
-            if row[link] is not None:
-                ox, oz = row[link]
-                source = ((ox - ux) % NX, (oz - uz) % NZ)
-                assert when[source] < step
-                for chunk in range(len(CHUNKS)):
-                    queue.append((source, when[source], step, chunk))
-        queues.append(queue)
-    return queues
+SENT = (
+    (
+        64, 65, 66, 120, 128, 121, 129, 130, 112, 113, 184, 114, 185, 144, 145, 146,
+        176, 178, 153, 154, 170,
+    ),
+    (
+        192, 193, 194, 200, 201, 202, 248, 250, 136, 137, 138, 208, 186, 232, 233, 18,
+        234, 177, 168, 169, 24, 25, 26, 161,
+    ),
+    (
+        8, 9, 10, 72, 73, 74, 16, 17, 80, 81, 82, 209, 210, 88, 89, 90,
+        216, 217, 152, 218, 96, 98, 160, 162,
+    ),
+    (
+        56, 57, 58, 48, 49, 50, 249, 122, 40, 41, 42, 240, 241, 242, 104, 105,
+        106, 32, 224, 225, 97, 226, 33, 34,
+    ),
+)
+TURNS = (
+    64, 192, 8, 56, -1, 65, 193, 9, 57, 66, 194, 10, 58, -9, -25, -2,
+    -8, 72, 200, 120, 48, 73, 201, 49, 128, 74, 202, 121, 50, -10, 16, 248,
+    129, 249, -26, 17, -7, 250, 130, 122, -32, 80, 136, 112, 40, -17, 81, 137,
+    113, 41, -16, 82, 138, 42, 184, -11, 209, -18, 208, 114, 240, 210, -6, 186,
+    185, 241, -15, 88, -27, 232, 242, 144, 89, -24, 233, 145, 104, 90, 18, 146,
+    105, -31, -12, 216, 234, 106, 176, -3, 217, 177, 178, 32, -19, -30, 168, 224,
+    152, 153, -14, 169, 225, 218, 154, -23, 24, 97, 96, -28, -20, 25, 170, 226,
+    98, -22, -29, 26, 33, -13, -4, 34, 160, -5, 161, 162, -21,
+)
 
 
 def kernel(
@@ -117,32 +116,35 @@
 
     neighbour = [device(sign * ux, 0, sign * uz, 0) for ux, uz in LINKS]
     twin = device(0, 0, 0, 1)
-    queues = plan()
     heads = [0] * len(LINKS)
-
-    def send_ready(done_step, done_chunk):
+    here = {chunk for chunk in range(len(CHUNKS))}
+
+    def spot(offset, chunk):
+        start, size = CHUNKS[chunk]
+        b = block(offset, sign, core)
+        return slots.at[b // 2, rows_of(b, start, size)]
+
+    def send_ready():
         progress = True
         while progress:
             progress = False
-            for link in range(len(LINKS)):
-                if heads[link] < len(queues[link]):
-                    source, came, step, chunk = queues[link][heads[link]]
-                    if (came, chunk) <= (done_step, done_chunk) or came < 0:
-                        start, size = CHUNKS[chunk]
-                        b = block(source, sign, core)
-                        here = slots.at[b // 2, rows_of(b, start, size)]
-                        src = factors.at[pl.ds(start, size)] if came < 0 else here
+            for link, (ux, uz) in enumerate(LINKS):
+                if heads[link] < len(SENT[link]):
+                    code = SENT[link][heads[link]]
+                    dx, dz, chunk = code // 64, code // 8 % 8, code % 8
+                    dx, dz = (dx - ux) % NX, (dz - uz) % NZ
+                    if 64 * dx + 8 * dz + chunk in here:
+                        dst = spot((dx, dz), chunk)
+                        src = factors.at[pl.ds(*CHUNKS[chunk])] if dx == dz == 0 else dst
                         remote(
-                            src, here, send_sem.at[0],
-                            ring_sem.at[(step * len(LINKS) + link) * len(CHUNKS) + chunk],
-                            neighbour[link],
+                            src, dst, send_sem.at[0], ring_sem.at[code], neighbour[link]
                         ).start()
                         heads[link] += 1
                         progress = True
 
-    send_ready(-1, len(CHUNKS))
-
-    order = [(0, 0)] + [offset for row_of in STEPS for offset in row_of if offset is not None]
+    send_ready()
+
+    order = [((-1 - turn) // 8, (-1 - turn) % 8) for turn in TURNS if turn < 0]
 
     def lend(indices):
         for k in indices:
@@ -155,7 +157,7 @@
                         send_sem.at[1], twin_sem.at[k], twin,
                     ).start()
 
-    lend(range(0, 9))
+    lend(range(AHEAD))
     remote(slab_in, twin_slab, send_sem.at[2], slab_sem, twin).start()
 
     blank = jnp.zeros((16, LANES), jnp.bfloat16)
@@ -174,45 +176,28 @@
     load_weights.wait()
     turned[:, 0:ROWS] = slab[...].T
 
-    def multiply(first, offsets):
-        blocks = [block(offset, sign, core) for offset in offsets]
-        for k in range(len(blocks)):
-            ref = twins.at[first + k]
-            pltpu.make_async_copy(ref, ref, twin_sem.at[first + k]).wait()
-
-        def one(j, carry):
-            b = blocks[0]
-            for k in range(1, len(blocks)):
-                b = jnp.where(j == k, blocks[k], b)
-            left = jnp.concatenate([costs[:, pl.ds(column(b), SLOT)], twins[first + j]], axis=0)
-            total[...] += jnp.dot(left, slots[b // 2], preferred_element_type=jnp.float32)
-            return carry
-
-        lax.fori_loop(0, len(blocks), one, 0)
-
-    ready, first = [(0, 0)], 0
-    for step, offsets in enumerate(STEPS):
-        for chunk, (start, size) in enumerate(CHUNKS):
-            for link, offset in enumerate(offsets):
-                if offset is not None:
-                    b = block(offset, sign, core)
-                    ref = slots.at[b // 2, rows_of(b, start, size)]
-                    remote(
-                        ref, ref, send_sem.at[0],
-                        ring_sem.at[(step * len(LINKS) + link) * len(CHUNKS) + chunk],
-                        neighbour[link],
-                    ).wait_recv()
-            send_ready(step, chunk)
-            if chunk == 0:
-                lend(range(4 * step + 9, 4 * step + 13))
-                if step == 0:
-                    load_own.wait()
-                    load_first.wait()
-                    load_second.wait()
-                multiply(first, ready)
-                first += len(ready)
-        ready = [offset for offset in offsets if offset is not None]
-    multiply(first, ready)
+    def multiply(k):
+        lend(range(k + AHEAD, k + AHEAD + 1))
+        if k == 0:
+            load_own.wait()
+            load_first.wait()
+            load_second.wait()
+        b = block(order[k], sign, core)
+        ref = twins.at[k]
+        pltpu.make_async_copy(ref, ref, twin_sem.at[k]).wait()
+        left = jnp.concatenate([costs[:, pl.ds(column(b), SLOT)], ref[...]], axis=0)
+        total[...] += jnp.dot(left, slots[b // 2], preferred_element_type=jnp.float32)
+
+    done = 0
+    for turn in TURNS:
+        if turn < 0:
+            multiply(done)
+            done += 1
+        else:
+            chunk = spot((turn // 64, turn // 8 % 8), turn % 8)
+            remote(chunk, chunk, send_sem.at[0], ring_sem.at[turn], neighbour[0]).wait_recv()
+            here.add(turn)
+            send_ready()
 
     half = lax.broadcasted_iota(jnp.int32, (1, LANES), 1) < RANK
     scale = 1.0 / (16.0 * math.sqrt(N))
@@ -239,12 +224,6 @@
             stat.at[pl.ds(pl.multiple_of(8 * g, 8), 8)], scattered.at[me],
             small_send.at[0], scatter_sem.at[0], to,
         ).start()
-    hand.wait()
-    prods[y] = halves[0] + halves[1]
-    for dy in (2, 1, 3):
-        remote(
-            prods.at[y], prods.at[y], small_send.at[2], prod_sem.at[0], device(0, dy, 0, 0)
-        ).start()
     seven = scattered.at[pl.ds(0, len(pairs))]
     pltpu.make_async_copy(seven, seven, scatter_sem.at[0]).wait()
     piece = scattered[0]
@@ -258,6 +237,12 @@
         remote(
             crossed.at[place], crossed.at[place], small_send.at[1], cross_sem.at[0],
             device(dx, 0, dz, 0),
+        ).start()
+    hand.wait()
+    prods[y] = halves[0] + halves[1]
+    for dy in (2, 1, 3):
+        remote(
+            prods.at[y], prods.at[y], small_send.at[2], prod_sem.at[0], device(0, dy, 0, 0)
         ).start()
     others = crossed.at[pl.ds(0, len(far))]
     pltpu.make_async_copy(others, others, cross_sem.at[0]).wait()
@@ -358,7 +343,7 @@
             dma((4,)),
             dma,
             dma((3,)),
-            dma((len(STEPS) * len(LINKS) * len(CHUNKS),)),
+            dma((8 * NX * NZ,)),
             dma((NX * NZ,)),
             dma,
             dma,

time: 58.7 us -> 57.6 us (0.981)
  Pallas kernels: 57.9 us -> 56.9 us
    pallas_call x1, Pallas kernels: 57.3 us -> 56.2 us  [local(): pl.pallas_call(kernel, out_shape=tuple((pltpu.VMEM(shape.shape, shape.dty...]
where the time goes in v3:
time: 57.6 us; the launch traced here: 57.5 us
  Pallas kernels  56.9 us (99%)
  between operations  0.64 us (1%)
    pallas_call x1, Pallas kernels, local(): pl.pallas_call(kernel, out_shape=tuple((pltpu.VMEM(shape.shape, shape.dty...  56.2 us

profile of v3, /device:TPU:1, one launch (start us, length us, event | category | flops | bytes accessed | tf_op | source)
XLA Modules:
  0.0 57.5 jit_solution(15688200094358377366)
XLA Ops:
  0.6 56.2 %shard_map.68 = (f32[128,128]{1,0:T(8,128)S(1)}, f32[1,64]{1,0:T(1,128)S(1)}) custom-call(bf16[128,25600]{1,0:T(8,128)(2,1)} %cost_first.1, bf16[128,25600]{1,0:T(8,128)(2,1)} %cost_second.1, bf16[400,128]{1,0:T(8,128)(2,1)} %factors.1, f32[128,128]{1,0:T(8,128)} %slab_in.1, f32[1,64]{1,0:T(1,128)} %bitcast.2), custom_call_target="tpu_custom_call" | custom-call | tf_op jit(solution)/shard_map/pallas_call | solution.py:321
  56.9 0.7 %shard_map.69 = (f32[128,128]{1,0:T(8,128)}, f32[1,64]{1,0:T(1,128)}) custom-call(f32[128,128]{1,0:T(8,128)S(1)} %get-tuple-element.6.new_in, f32[1,64]{1,0:T(1,128)S(1)} %get-tuple-element.7.marginal_in), custom_call_target="tpu_custom_call" | custom-call | tf_op jit(solution)/shard_map/pallas_call | solution.py:361

commit v4 on v3

--- a/solution.py
+++ b/solution.py
@@ -22,34 +22,36 @@
 
 AHEAD = 9
 LINKS = ((1, 0), (-1, 0), (0, 1), (0, -1))
-CHUNKS = ((0, 144), (144, 128), (272, 128))
+CHUNKS = ((0, 112), (112, 96), (208, 96), (304, 96))
 SENT = (
     (
-        64, 65, 66, 120, 128, 121, 129, 130, 112, 113, 184, 114, 185, 144, 145, 146,
-        176, 178, 153, 154, 170,
+        65, 67, 66, 64, 122, 123, 72, 120, 75, 128, 137, 80, 136, 82, 138, 83,
+        112, 144, 139, 89, 90, 107, 91, 177, 186, 99, 42, 98, 97, 131, 130,
     ),
     (
-        192, 193, 194, 200, 201, 202, 248, 250, 136, 137, 138, 208, 186, 232, 233, 18,
-        234, 177, 168, 169, 24, 25, 26, 161,
+        193, 194, 192, 195, 250, 200, 248, 203, 129, 201, 242, 243, 208, 210, 209, 240,
+        241, 178, 179, 217, 146, 147, 176, 170, 218, 187, 224, 225, 168, 169, 163,
     ),
     (
-        8, 9, 10, 72, 73, 74, 16, 17, 80, 81, 82, 209, 210, 88, 89, 90,
-        216, 217, 152, 218, 96, 98, 160, 162,
+        8, 10, 9, 11, 73, 16, 17, 18, 74, 19, 202, 81, 24, 25, 26, 211,
+        27, 145, 88, 32, 33, 34, 216, 153, 152, 96, 154, 155, 219, 161, 160,
     ),
     (
-        56, 57, 58, 48, 49, 50, 249, 122, 40, 41, 42, 240, 241, 242, 104, 105,
-        106, 32, 224, 225, 97, 226, 33, 34,
+        58, 59, 56, 57, 50, 51, 249, 121, 251, 48, 49, 114, 43, 115, 113, 185,
+        184, 234, 235, 35, 40, 41, 232, 233, 227, 171, 104, 226, 105, 106, 162,
     ),
 )
 TURNS = (
-    64, 192, 8, 56, -1, 65, 193, 9, 57, 66, 194, 10, 58, -9, -25, -2,
-    -8, 72, 200, 120, 48, 73, 201, 49, 128, 74, 202, 121, 50, -10, 16, 248,
-    129, 249, -26, 17, -7, 250, 130, 122, -32, 80, 136, 112, 40, -17, 81, 137,
-    113, 41, -16, 82, 138, 42, 184, -11, 209, -18, 208, 114, 240, 210, -6, 186,
-    185, 241, -15, 88, -27, 232, 242, 144, 89, -24, 233, 145, 104, 90, 18, 146,
-    105, -31, -12, 216, 234, 106, 176, -3, 217, 177, 178, 32, -19, -30, 168, 224,
-    152, 153, -14, 169, 225, 218, 154, -23, 24, 97, 96, -28, -20, 25, 170, 226,
-    98, -22, -29, 26, 33, -13, -4, 34, 160, -5, 161, 162, -21,
+    65, 193, 58, 8, 67, 194, 59, 10, 66, 192, 9, 56, 64, 195, 11, 57,
+    -1, -9, -25, -2, -8, 73, 122, 250, 50, 16, 123, 51, 200, 17, 72, 249,
+    248, 18, 121, 120, 203, 74, 251, 75, -16, 129, -32, 19, 48, 128, 201, 202,
+    49, 137, 242, 81, 114, -10, 80, 243, 24, 43, 136, 208, -3, 25, 115, 82,
+    210, 26, 113, 138, 209, -26, 211, 185, -7, 83, 240, 27, 184, -27, 112, 241,
+    145, 234, 178, 144, 88, 235, -11, 179, 139, 35, 32, 217, 89, -4, 33, 40,
+    146, 90, -15, 34, 41, 147, 107, -31, 216, 232, 176, 91, -18, 153, 233, 170,
+    177, -5, -19, 152, 227, 218, 186, -12, -30, 171, 96, 187, 99, -23, -24, 104,
+    42, 224, 154, -6, 226, 98, 225, 155, -29, -20, 105, 97, 219, 168, -13, -28,
+    106, 131, 161, 169, -14, -22, 162, 130, -17, 163, 160, -21,
 )
 
 
@@ -74,18 +76,28 @@
         cc = lax.rem(core + dc, 2)
         return ((xx * NZ + zz) * 2 + cc, yy)
 
-    def block(offset, way, c):
-        ox, oz = offset
-        ox, oz = (ox - NX if ox > NX // 2 else ox), (oz - NZ if oz > NZ // 2 else oz)
-        xx = lax.rem(x - way * ox + NX, NX)
-        zz = lax.rem(z - way * oz + NZ, NZ)
-        return (xx * NZ + zz) * 2 + c
-
-    def rows_of(b, start, size):
-        return pl.ds(pl.multiple_of(16 * lax.rem(b, 8) + start, 16), size)
-
-    def column(b):
-        return pl.multiple_of(DEEP * b - 16 * lax.rem(b, 8), 128)
+    def signed(step, ring):
+        return step - ring if step > ring // 2 else step
+
+    where_x, where_z, shift_z = {}, {}, {}
+    for away in (False, True):
+        way, c = (-sign, 1 - core) if away else (sign, core)
+        for dx in range(NX):
+            where_x[away, dx] = lax.rem(x - way * signed(dx, NX) + NX, NX) * NZ
+        for dz in range(NZ):
+            where_z[away, dz] = lax.rem(z - way * signed(dz, NZ) + NZ, NZ)
+            shift_z[away, dz] = 16 * lax.rem(2 * where_z[away, dz] + c, 8)
+
+    def home(offset, away=False):
+        return where_x[away, offset[0]] + where_z[away, offset[1]]
+
+    def span(offset, start, size):
+        return pl.ds(pl.multiple_of(shift_z[False, offset[1]] + start, 16), size)
+
+    def column(offset, away):
+        c = 1 - core if away else core
+        first = 2 * DEEP * home(offset, away) + DEEP * c - shift_z[away, offset[1]]
+        return pl.ds(pl.multiple_of(first, 128), SLOT)
 
     def remote(src, dst, send, recv, to):
         return pltpu.make_async_remote_copy(
@@ -96,13 +108,13 @@
     load_first = pltpu.make_async_copy(cost_first, costs.at[pl.ds(0, ROWS)], load_sem.at[0])
     load_second = pltpu.make_async_copy(cost_second, costs.at[pl.ds(ROWS, ROWS)], load_sem.at[1])
     place = x * NZ + z
-    own_slot = slots.at[place, rows_of(row, 0, DEEP)]
+    own_slot = slots.at[place, span((0, 0), 0, DEEP)]
     load_own = pltpu.make_async_copy(factors, own_slot, own_sem)
     load_slab = pltpu.make_async_copy(slab_in, slab, load_sem.at[2])
     load_weights = pltpu.make_async_copy(weights_in, weights, load_sem.at[3])
 
     barrier = pltpu.get_barrier_semaphore()
-    pairs = [(dy, dc) for dy in range(NY) for dc in range(2) if (dy, dc) != (0, 0)]
+    pairs = [(dy, dc) for dy in (2, 1, 3, 0) for dc in (1, 0) if (dy, dc) != (0, 0)]
     greeted = [device(ux, 0, uz, 0) for ux, uz in LINKS]
     greeted += [device(0, dy, 0, dc) for dy, dc in pairs]
     for to in greeted:
@@ -121,8 +133,7 @@
 
     def spot(offset, chunk):
         start, size = CHUNKS[chunk]
-        b = block(offset, sign, core)
-        return slots.at[b // 2, rows_of(b, start, size)]
+        return slots.at[home(offset), span(offset, start, size)]
 
     def send_ready():
         progress = True
@@ -149,8 +160,7 @@
     def lend(indices):
         for k in indices:
             if k < len(order):
-                b = block(order[k], -sign, 1 - core)
-                at = pl.ds(column(b), SLOT)
+                at = column(order[k], True)
                 for part, cost in enumerate((cost_first, cost_second)):
                     remote(
                         cost.at[:, at], twins.at[k, pl.ds(part * ROWS, ROWS)],
@@ -172,9 +182,6 @@
 
     lax.fori_loop(0, NX * NZ // 4, clear, 0)
     total[...] = jnp.zeros_like(total)
-    load_slab.wait()
-    load_weights.wait()
-    turned[:, 0:ROWS] = slab[...].T
 
     def multiply(k):
         lend(range(k + AHEAD, k + AHEAD + 1))
@@ -182,17 +189,27 @@
             load_own.wait()
             load_first.wait()
             load_second.wait()
-        b = block(order[k], sign, core)
         ref = twins.at[k]
         pltpu.make_async_copy(ref, ref, twin_sem.at[k]).wait()
-        left = jnp.concatenate([costs[:, pl.ds(column(b), SLOT)], ref[...]], axis=0)
-        total[...] += jnp.dot(left, slots[b // 2], preferred_element_type=jnp.float32)
+        left = jnp.concatenate([costs[:, column(order[k], False)], ref[...]], axis=0)
+        total[...] += jnp.dot(left, slots[home(order[k])], preferred_element_type=jnp.float32)
+
+    def split():
+        load_slab.wait()
+        load_weights.wait()
+        remote(slab_in, twin_slab, send_sem.at[2], slab_sem, twin).wait_recv()
+        rest = jnp.concatenate([slab[...].T, twin_slab[...].T], axis=1)
+        for part in range(3):
+            turned[pl.ds(part * LANES, LANES), :] = rest.astype(jnp.bfloat16)
+            rest = rest - rest.astype(jnp.bfloat16).astype(jnp.float32)
 
     done = 0
     for turn in TURNS:
         if turn < 0:
             multiply(done)
             done += 1
+            if done == 12:
+                split()
         else:
             chunk = spot((turn // 64, turn // 8 % 8), turn % 8)
             remote(chunk, chunk, send_sem.at[0], ring_sem.at[turn], neighbour[0]).wait_recv()
@@ -203,16 +220,19 @@
     scale = 1.0 / (16.0 * math.sqrt(N))
     part = jnp.where(half, total[0:ROWS, :], total[ROWS : 2 * ROWS, :]) * scale
     lent = jnp.where(half, total[2 * ROWS : 3 * ROWS, :], total[3 * ROWS :, :]) * scale
-    outgoing[...] = lent
-    hand = remote(outgoing, halves.at[core], small_send.at[5], half_sem, twin)
-    hand.start()
-    halves[core] = part
-    remote(slab_in, twin_slab, send_sem.at[2], slab_sem, twin).wait_recv()
-    turned[:, ROWS:] = twin_slab[...].T
-    terms = jnp.dot(
-        turned[...], jnp.concatenate([part, lent], axis=0), precision=HIGH,
-        preferred_element_type=jnp.float32,
-    )
+    rest = jnp.concatenate([part, lent], axis=0)
+    pairs_of = []
+    for count in (3, 2, 1):
+        piece = rest.astype(jnp.bfloat16)
+        rest = rest - piece.astype(jnp.float32)
+        pairs_of.append(
+            jnp.dot(
+                turned[0 : count * LANES, :], piece, preferred_element_type=jnp.float32
+            )
+        )
+    one, two, three = pairs_of
+    small = one[2 * LANES :] + two[LANES:] + three
+    terms = one[0:LANES] + ((one[LANES : 2 * LANES] + two[0:LANES]) + small)
     stat[...] = jnp.where(half, terms[0:RANK, :], terms[RANK:, :])
 
     me = y * 2 + core
@@ -224,6 +244,10 @@
             stat.at[pl.ds(pl.multiple_of(8 * g, 8), 8)], scattered.at[me],
             small_send.at[0], scatter_sem.at[0], to,
         ).start()
+    outgoing[...] = lent
+    hand = remote(outgoing, halves.at[core], small_send.at[5], half_sem, twin)
+    hand.start()
+    halves[core] = part
     seven = scattered.at[pl.ds(0, len(pairs))]
     pltpu.make_async_copy(seven, seven, scatter_sem.at[0]).wait()
     piece = scattered[0]
@@ -331,7 +355,7 @@
             pltpu.VMEM((NX * NZ, 2 * ROWS, SLOT), bf16),
             pltpu.VMEM((NX * NZ, SLOT, LANES), bf16),
             pltpu.VMEM((4 * ROWS, LANES), f32),
-            pltpu.VMEM((LANES, 2 * ROWS), f32),
+            pltpu.VMEM((3 * LANES, 2 * ROWS), bf16),
             pltpu.VMEM((2, ROWS, LANES), f32),
             pltpu.VMEM((ROWS, LANES), f32),
             pltpu.VMEM((NY, ROWS, LANES), f32),

time: 57.6 us -> 56.4 us (0.979)
  Pallas kernels: 56.9 us -> 55.7 us
    pallas_call x1, Pallas kernels: 56.2 us -> 55 us  [local(): pl.pallas_call(kernel, out_shape=tuple((pltpu.VMEM(shape.shape, shape.dty...]
where the time goes in v4:
time: 56.4 us; the launch traced here: 56.3 us
  Pallas kernels  55.7 us (99%)
  between operations  0.64 us (1%)
    pallas_call x1, Pallas kernels, local(): pl.pallas_call(kernel, out_shape=tuple((pltpu.VMEM(shape.shape, shape.dty...  55 us

profile of v4, /device:TPU:1, one launch (start us, length us, event | category | flops | bytes accessed | tf_op | source)
XLA Modules:
  0.0 56.3 jit_solution(8810372318217153974)
XLA Ops:
  0.6 55.0 %shard_map.68 = (f32[128,128]{1,0:T(8,128)S(1)}, f32[1,64]{1,0:T(1,128)S(1)}) custom-call(bf16[128,25600]{1,0:T(8,128)(2,1)} %cost_first.1, bf16[128,25600]{1,0:T(8,128)(2,1)} %cost_second.1, bf16[400,128]{1,0:T(8,128)(2,1)} %factors.1, f32[128,128]{1,0:T(8,128)} %slab_in.1, f32[1,64]{1,0:T(1,128)} %bitcast.2), custom_call_target="tpu_custom_call" | custom-call | tf_op jit(solution)/shard_map/pallas_call | solution.py:345
  55.7 0.7 %shard_map.69 = (f32[128,128]{1,0:T(8,128)}, f32[1,64]{1,0:T(1,128)}) custom-call(f32[128,128]{1,0:T(8,128)S(1)} %get-tuple-element.6.new_in, f32[1,64]{1,0:T(1,128)S(1)} %get-tuple-element.7.marginal_in), custom_call_target="tpu_custom_call" | custom-call | tf_op jit(solution)/shard_map/pallas_call | solution.py:385

commit v5 on v4

--- a/solution.py
+++ b/solution.py
@@ -25,33 +25,33 @@
 CHUNKS = ((0, 112), (112, 96), (208, 96), (304, 96))
 SENT = (
     (
-        65, 67, 66, 64, 122, 123, 72, 120, 75, 128, 137, 80, 136, 82, 138, 83,
-        112, 144, 139, 89, 90, 107, 91, 177, 186, 99, 42, 98, 97, 131, 130,
+        67, 66, 64, 65, 131, 130, 72, 120, 128, 121, 139, 80, 136, 184, 138, 113,
+        186, 144, 106, 147, 90, 89, 107, 81, 98, 170, 155, 154, 153, 163, 162,
     ),
     (
-        193, 194, 192, 195, 250, 200, 248, 203, 129, 201, 242, 243, 208, 210, 209, 240,
-        241, 178, 179, 217, 146, 147, 176, 170, 218, 187, 224, 225, 168, 169, 163,
+        193, 194, 195, 192, 129, 200, 248, 203, 202, 250, 185, 242, 201, 243, 241, 210,
+        209, 211, 123, 137, 216, 235, 234, 232, 219, 226, 233, 145, 171, 218, 225,
     ),
     (
-        8, 10, 9, 11, 73, 16, 17, 18, 74, 19, 202, 81, 24, 25, 26, 211,
-        27, 145, 88, 32, 33, 34, 216, 153, 152, 96, 154, 155, 219, 161, 160,
+        8, 11, 10, 9, 75, 16, 74, 18, 73, 17, 19, 83, 208, 24, 26, 25,
+        27, 91, 88, 82, 32, 146, 33, 99, 152, 114, 96, 224, 217, 97, 160,
     ),
     (
-        58, 59, 56, 57, 50, 51, 249, 121, 251, 48, 49, 114, 43, 115, 113, 185,
-        184, 234, 235, 35, 40, 41, 232, 233, 227, 171, 104, 226, 105, 106, 162,
+        58, 56, 59, 57, 249, 50, 251, 51, 49, 48, 122, 187, 42, 240, 43, 112,
+        40, 177, 34, 41, 35, 176, 104, 169, 105, 115, 179, 178, 168, 227, 161,
     ),
 )
 TURNS = (
-    65, 193, 58, 8, 67, 194, 59, 10, 66, 192, 9, 56, 64, 195, 11, 57,
-    -1, -9, -25, -2, -8, 73, 122, 250, 50, 16, 123, 51, 200, 17, 72, 249,
-    248, 18, 121, 120, 203, 74, 251, 75, -16, 129, -32, 19, 48, 128, 201, 202,
-    49, 137, 242, 81, 114, -10, 80, 243, 24, 43, 136, 208, -3, 25, 115, 82,
-    210, 26, 113, 138, 209, -26, 211, 185, -7, 83, 240, 27, 184, -27, 112, 241,
-    145, 234, 178, 144, 88, 235, -11, 179, 139, 35, 32, 217, 89, -4, 33, 40,
-    146, 90, -15, 34, 41, 147, 107, -31, 216, 232, 176, 91, -18, 153, 233, 170,
-    177, -5, -19, 152, 227, 218, 186, -12, -30, 171, 96, 187, 99, -23, -24, 104,
-    42, 224, 154, -6, 226, 98, 225, 155, -29, -20, 105, 97, 219, 168, -13, -28,
-    106, 131, 161, 169, -14, -22, 162, 130, -17, 163, 160, -21,
+    67, 193, 58, 8, 66, 194, 11, 56, -1, 195, 64, 10, 59, 65, 192, 9,
+    57, -9, -25, -2, -8, 131, 75, 129, 249, 130, 16, 50, 200, 72, 74, 251,
+    248, 18, 120, 51, 203, 73, 49, 128, 202, -10, 17, 121, 48, 250, -17, 19,
+    122, 139, 185, -7, 83, 187, 80, 242, 208, 42, 201, 136, -32, 24, 240, 243,
+    184, -3, 26, 43, 241, 138, -26, 25, 112, 210, 113, -31, 27, 40, 209, 186,
+    -4, 91, 177, 211, 144, -24, 88, 34, 123, 106, 82, 41, 137, 147, -27, -16,
+    32, 35, 216, 90, -6, 146, 235, 89, 176, 33, 234, 107, 104, -18, -12, 99,
+    81, 232, 169, -5, -11, 152, 98, 219, 105, -14, 114, 170, 226, 115, -15, 155,
+    233, 96, 179, -30, 154, 145, 178, 224, -19, -23, 153, 171, 217, 168, -20, -22,
+    218, 163, 97, 227, -28, -13, 225, -29, 161, 160, 162, -21,
 )
 
 
@@ -254,21 +254,32 @@
     for g in range(1, 8):
         piece = piece + scattered[g]
     crossed[place] = piece
-    far = [
-        (dx, dz) for dz in (4, 3, 5, 2, 6, 1, 7, 0) for dx in (2, 1, 3, 0) if (dx, dz) != (0, 0)
-    ]
-    for dx, dz in far:
+
+    def farthest_first(send):
+        def one(i, carry):
+            dz = NZ // 2 + (i + 1) // 2 * (1 - 2 * lax.rem(i, 2))
+            for dx in (2, 1, 3, 0):
+                send(dx, dz)
+            return carry
+
+        lax.fori_loop(0, NZ - 1, one, 0)
+        for dx in (2, 1, 3):
+            send(dx, 0)
+
+    def send_piece(dx, dz):
         remote(
             crossed.at[place], crossed.at[place], small_send.at[1], cross_sem.at[0],
             device(dx, 0, dz, 0),
         ).start()
+
+    farthest_first(send_piece)
     hand.wait()
     prods[y] = halves[0] + halves[1]
     for dy in (2, 1, 3):
         remote(
             prods.at[y], prods.at[y], small_send.at[2], prod_sem.at[0], device(0, dy, 0, 0)
         ).start()
-    others = crossed.at[pl.ds(0, len(far))]
+    others = crossed.at[pl.ds(0, NX * NZ - 1)]
     pltpu.make_async_copy(others, others, cross_sem.at[0]).wait()
     piece = jnp.sum(crossed[...], axis=0)
     mine_rows = pl.ds(pl.multiple_of(8 * me, 8), 8)
@@ -300,13 +311,16 @@
     high = jnp.sum(jnp.where(half, 0.0, tilde), axis=1, keepdims=True)
     result = tilde / jnp.where(half, low, high)
     sums[row] = jnp.sum(result, axis=0, keepdims=True)
-    for dx, dz in far + [(0, 0)]:
+
+    def send_sums(dx, dz):
         for dc in (0, 1):
-            if (dx, dz, dc) != (0, 0, 0):
-                remote(
-                    sums.at[row], sums.at[row], small_send.at[4], sum_sem.at[0],
-                    device(dx, 0, dz, dc),
-                ).start()
+            remote(
+                sums.at[row], sums.at[row], small_send.at[4], sum_sem.at[0],
+                device(dx, 0, dz, dc),
+            ).start()
+
+    farthest_first(send_sums)
+    remote(sums.at[row], sums.at[row], small_send.at[4], sum_sem.at[0], twin).start()
     new[...] = result
 
     rest = sums.at[pl.ds(0, BLOCKS - 1)]

time: 56.4 us -> 56.4 us (level)
  no operation moved by 1% of the time
where the time goes in v5:
time: 56.4 us; the launch traced here: 56.3 us
  Pallas kernels  55.7 us (99%)
  between operations  0.64 us (1%)
    pallas_call x1, Pallas kernels, local(): pl.pallas_call(kernel, out_shape=tuple((pltpu.VMEM(shape.shape, shape.dty...  55 us

profile of v5, /device:TPU:1, one launch (start us, length us, event | category | flops | bytes accessed | tf_op | source)
XLA Modules:
  0.0 56.3 jit_solution(803380778536928759)
XLA Ops:
  0.6 55.0 %shard_map.68 = (f32[128,128]{1,0:T(8,128)S(1)}, f32[1,64]{1,0:T(1,128)S(1)}) custom-call(bf16[128,25600]{1,0:T(8,128)(2,1)} %cost_first.1, bf16[128,25600]{1,0:T(8,128)(2,1)} %cost_second.1, bf16[400,128]{1,0:T(8,128)(2,1)} %factors.1, f32[128,128]{1,0:T(8,128)} %slab_in.1, f32[1,64]{1,0:T(1,128)} %bitcast.2), custom_call_target="tpu_custom_call" | custom-call | tf_op jit(solution)/shard_map/pallas_call | solution.py:359
  55.7 0.7 %shard_map.69 = (f32[128,128]{1,0:T(8,128)}, f32[1,64]{1,0:T(1,128)}) custom-call(f32[128,128]{1,0:T(8,128)S(1)} %get-tuple-element.6.new_in, f32[1,64]{1,0:T(1,128)S(1)} %get-tuple-element.7.marginal_in), custom_call_target="tpu_custom_call" | custom-call | tf_op jit(solution)/shard_map/pallas_call | solution.py:399
